TPU v7x, 512 devices: a whole 4x4x16 slice. The times are simulated.
512 devices in a mesh: sensor: 64 (over z, y), slot: 4 (over x_hi, core), day: 2 (over x_lo).
Axes of the slice: x: 4 (x_hi: 2, x_lo: 2; x = x_hi * 2 + x_lo), y: 4, z: 16, core: 2. Of those that a mesh axis runs over, the one named last changes fastest.
Arguments:
- traffic: float32 [10, 288, 204800], P('day', 'slot', 'sensor'), may hold values from -1400 to 1400
- slot_factor: float32 [288, 128], replicated, may hold values from -6 to 6
- day_factor: float32 [10, 128], replicated, may hold values from -6 to 6
Outputs:
- sensor_factor: float32 [204800, 128], P(('sensor', 'slot', 'day'))
- slot_factor_new: float32 [288, 128], P('slot')
- day_factor_new: float32 [10, 128], P('day')
All inputs are finite; a program needn't handle non-finite values.
Results may differ from a plain program's by a relative error of at most 0.0003.
Values sent between devices are 32-bit elements; how exact they have to be, the bound alone decides.
A program may use at most 64 MiB of HBM per device.

v0:
```python
import jax
import jax.numpy as jnp
from jax import lax
from jax.sharding import PartitionSpec as P

highest = lax.Precision.HIGHEST
ridge_scale = 0.001
epsilon = 1e-05


def gram_of(factor_rows):
    return jnp.einsum("ir,is->rs", factor_rows, factor_rows, precision=highest)


def regularize(matrix):
    order_count = matrix.shape[0]
    diag_mean = jnp.mean(jnp.diagonal(matrix))
    return matrix + ridge_scale * diag_mean * jnp.eye(order_count, dtype=matrix.dtype)


def solve_rows(right_side, normal_matrix):
    lower_factor = jnp.linalg.cholesky(normal_matrix)
    halfway = lax.linalg.triangular_solve(
        lower_factor, right_side, left_side=False, lower=True, transpose_a=True
    )
    return lax.linalg.triangular_solve(
        lower_factor, halfway, left_side=False, lower=True, transpose_a=False
    )


def normalize(raw_gram, row_count):
    norms = jnp.sqrt(jnp.diagonal(raw_gram) / row_count + epsilon)
    return (norms, raw_gram / (norms[:, None] * norms[None, :]))


def on_device(traffic, slot_factor, day_factor):
    day_rows, slot_rows, sensor_rows = traffic.shape
    slot_count = slot_factor.shape[0]
    sensor_count = sensor_rows * lax.axis_size("sensor")
    group_count = lax.axis_size("slot") * lax.axis_size("day")
    own_rows = sensor_rows // group_count
    slot_index = lax.axis_index("slot")
    day_index = lax.axis_index("day")
    slot_local = lax.dynamic_slice_in_dim(slot_factor, slot_index * slot_rows, slot_rows, 0)
    day_local = lax.dynamic_slice_in_dim(day_factor, day_index * day_rows, day_rows, 0)
    own_start = (slot_index * lax.axis_size("day") + day_index) * own_rows
    gram_slot = gram_of(slot_factor)
    gram_day = gram_of(day_factor)
    normal_sensor = regularize(gram_slot * gram_day)
    partial_value = jnp.einsum("kji,jr->kir", traffic, slot_local, precision=highest)
    block_rhs = lax.psum(
        jnp.einsum("kir,kr->ir", partial_value, day_local, precision=highest), ("slot", "day")
    )
    block_raw = solve_rows(block_rhs, normal_sensor)
    raw_gram = lax.psum(gram_of(block_raw), "sensor")
    sensor_norms, gram_sensor = normalize(raw_gram, sensor_count)
    block_factor = block_raw / sensor_norms[None, :]
    sensor_factor = lax.dynamic_slice_in_dim(block_factor, own_start, own_rows, 0)
    contracted = jnp.einsum("kji,ir->kjr", traffic, block_factor, precision=highest)
    slot_part = jnp.sum(contracted * day_local[:, None, :], axis=0)
    slot_rhs = lax.psum(slot_part, ("sensor", "day"))
    slot_raw = solve_rows(slot_rhs, regularize(gram_sensor * gram_day))
    local_gram = gram_of(slot_raw)
    slot_gram_raw = lax.psum(local_gram, "slot")
    slot_norms, gram_slot_new = normalize(slot_gram_raw, slot_count)
    slot_factor_new = slot_raw / slot_norms[None, :]
    day_part = jnp.sum(contracted * slot_factor_new[None, :, :], axis=1)
    day_rhs = lax.psum(day_part, ("sensor", "slot"))
    day_factor_new = solve_rows(day_rhs, regularize(gram_sensor * gram_slot_new))
    return (sensor_factor, slot_factor_new, day_factor_new)


def solution(mesh):
    in_specs = (P("day", "slot", "sensor"), P(), P())
    out_specs = (P(("sensor", "slot", "day"), None), P("slot", None), P("day", None))
    return jax.shard_map(
        on_device, mesh=mesh, in_specs=in_specs, out_specs=out_specs, check_vma=False
    )
```

profile of v0, /device:TPU:1, one launch (start us, length us, event | category | flops | bytes accessed | tf_op | source)
XLA Modules:
  0.0 1761.9 jit_solution(11763680636063976119)
XLA Ops:
  7.2 0.7 fusion.55
  8.0 0.1 copy.24
  8.1 9.3 convolution_bitcast_fusion
  17.4 17.7 %fusion = f32[128,1,3200]{2,1,0:T(1,128)S(1)} fusion(f32[5,128,1]{0,2,1:T(1,128)S(1)} %copy.24, f32[5,3200,128]{1,2,0:T(8,128)S(1)} %convolution_bitcast_fusion), kind=kOutput, calls=%fused_computation.5 | convolution fusion | flops 24576000 | bytes 9832960 | tf_op jit(solution)/shard_map/kir,kr->ir/dot_general | solution.py:52
  35.1 1.3 copy.30
  36.4 0.6 copy-done.5
  37.1 0.3 fusion.35
  37.4 0.6 copy-done.2
  38.0 0.5 convolution_multiply_fusion
  38.5 1.6 gather_fusion
  40.1 0.6 reduce_sum.45
  41.4 0.1 copy.18
  41.6 11.7 cholesky.59
  53.4 0.6 compare_reduce_fusion.2
  54.0 0.7 fusion.7
  54.7 9.8 custom-call.17
  64.5 55.5 %all-reduce.4.cloned.1.call-done = f32[3200,128]{0,1:T(8,128)} async-done(((f32[3200,128]{0,1:T(8,128)}), f32[3200,128]{0,1:T(8,128)}) %all-reduce.4.cloned.1.call-update) | async-done | bytes 1638416 | tf_op jit(solution)/shard_map/psum | solution.py:51
  120.1 4.2 fusion.22
  124.3 1.5 fusion.20
  125.8 3.6 fusion.36
  129.5 248.6 %all-reduce.6.cloned.1.call-done = f32[128,128]{1,0:T(8,128)} async-done(((f32[128,128]{1,0:T(8,128)}), f32[128,128]{1,0:T(8,128)}) %all-reduce.6.cloned.1.call-update) | async-done | bytes 65552 | tf_op jit(solution)/shard_map/psum | solution.py:55
  378.1 1.9 gather_fusion.1
  380.1 0.1 broadcast_divide_fusion
  380.2 6.2 multiply_reduce_fusion.1
  386.5 497.3 %psum.37 = f32[72,128]{1,0:T(8,128)S(1)} all-reduce(f32[72,128]{1,0:T(8,128)S(1)} %get-tuple-element.4), channel_id=1, replica_groups=mesh['sensor'=64,'slot'=4,'day'=2] {'sensor','day'}, use_global_device_ids=true, to_apply=%region_6.8 | all-reduce | flops 9216 | bytes 73728 | tf_op jit(solution)/shard_map/psum | solution.py:61
  883.8 0.1 fusion.33
  883.9 1.2 gather_fusion.2
  885.1 0.6 reduce_sum.47
  886.6 11.7 cholesky.70
  898.4 0.6 compare_reduce_fusion.1
  899.0 0.7 fusion.8
  899.7 9.8 custom-call.18
  909.5 0.2 fusion.17
  909.7 0.3 fusion.15
  910.0 0.9 fusion.37
  910.9 0.7 constant_dynamic-slice_fusion
  911.6 168.1 %all-reduce.8.cloned.1.call-done = f32[128,128]{1,0:T(8,128)} async-done(((f32[128,128]{1,0:T(8,128)}), f32[128,128]{1,0:T(8,128)}) %all-reduce.8.cloned.1.call-update) | async-done | bytes 65552 | tf_op jit(solution)/shard_map/psum | solution.py:64
  1079.7 1.9 gather_fusion.3
  1081.7 645.7 %psum.39 = f32[5,128]{1,0:T(8,128)S(1)} all-reduce(f32[5,128]{1,0:T(8,128)S(1)} %multiply_reduce_fusion), channel_id=1, replica_groups=mesh['sensor'=64,'slot'=4,'day'=2] {'sensor','slot'}, use_global_device_ids=true, to_apply=%region_10.12 | all-reduce | flops 640 | bytes 5120 | tf_op jit(solution)/shard_map/psum | solution.py:68
  1727.4 0.9 divide_multiply_fusion
  1728.3 1.5 gather_fusion.4
  1729.8 0.6 reduce_sum.49
  1731.3 11.7 cholesky.81
  1743.0 0.6 compare_reduce_fusion
  1743.7 0.7 fusion.9
  1744.3 9.8 custom-call.19
  1754.1 0.2 fusion.12
  1754.3 0.8 fusion.10
  (36 shorter events, 0.9 us)
Async XLA Ops:
  7.2 0.9 copy-start
  7.2 112.9 %all-reduce.4.cloned.1.call-start = ((), (), s32[]{:S(2)}) async-start(), calls=%async_computation | async-start | bytes 3276800 | tf_op jit(solution)/shard_map/psum | solution.py:51
  36.4 0.7 copy-start.5
  36.4 341.7 %all-reduce.6.cloned.1.call-start = ((), (), s32[]{:S(2)}) async-start(), calls=%async_computation.1 | async-start | bytes 131072 | tf_op jit(solution)/shard_map/psum | solution.py:55
  37.4 0.6 copy-start.2
  129.4 950.3 %all-reduce.8.cloned.1.call-start = ((), (), s32[]{:S(2)}) async-start(), calls=%async_computation.2 | async-start | bytes 131072 | tf_op jit(solution)/shard_map/psum | solution.py:64
  380.2 503.6 %copy-start.1 = (f32[128,128]{1,0:T(8,128)S(1)}, f32[128,128]{1,0:T(8,128)}, u32[]{:S(2)}) copy-start(f32[128,128]{1,0:T(8,128)} %all-reduce.6.cloned.1.call-done) | copy-start | bytes 196612
  380.2 503.6 %copy-start.3 = (f32[128,128]{1,0:T(8,128)S(1)}, f32[128,128]{1,0:T(8,128)}, u32[]{:S(2)}) copy-start(f32[128,128]{1,0:T(8,128)} %copy-done.2) | copy-start | bytes 196612
  1081.7 673.5 %copy-start.4 = (f32[72,128]{1,0:T(8,128)}, f32[72,128]{1,0:T(8,128)S(1)}, u32[]{:S(2)}) copy-start(f32[72,128]{1,0:T(8,128)S(1)} %broadcast_divide_fusion.1) | copy-start | bytes 110596
Sparse Core Ops, SparseCore 0:
  36.5 83.5 all-reduce.3
  129.5 248.5 all-reduce.5
  911.1 168.5 all-reduce.7
where the time goes:
time: 1770 us; the launch traced here: 1760 us
  blocking collectives  1140 us (64%)
  waiting for transfers between devices  472 us (27%)
  other arithmetic  71.7 us (4%)
  matrix products  45.7 us (3%)
    psum x1, blocking collectives, on_device(): day_rhs = lax.psum(day_part, ('sensor', 'slot'))  646 us
    psum x1, blocking collectives, on_device(): slot_rhs = lax.psum(slot_part, ('sensor', 'day'))  497 us
    psum x1, waiting for transfers between devices, on_device(): raw_gram = lax.psum(gram_of(block_raw), 'sensor')  249 us
    psum x1, waiting for transfers between devices, on_device(): slot_gram_raw = lax.psum(local_gram, 'slot')  168 us
    psum x1, waiting for transfers between devices, on_device(): lax.psum(jnp.einsum('kir,kr->ir', partial_value, day_local, precision=hig...  55.5 us
    another operation x9, other arithmetic, solve_rows(): lower_factor = jnp.linalg.cholesky(normal_matrix)  37.2 us
  transfers between devices with their start and end apart: 3, of which 3 were waited for; matrix products, arithmetic and copies ran while one was open for 2% of the time, Pallas kernels for 0%

commit v1 on v0

v1 whole, which is shorter than its diff:
```python
import jax
import jax.numpy as jnp
from jax import lax
from jax.experimental import pallas as pl
from jax.experimental.pallas import tpu as pltpu
from jax.sharding import PartitionSpec as P

MESH = pl.DeviceIdType.MESH
highest = lax.Precision.HIGHEST
f32 = jnp.float32
bf16 = jnp.bfloat16
ridge_scale = 0.001
epsilon = 1e-05

R = 128
NX, NY, NZ = 4, 4, 16
GROUP = 8
WINDOW, STRIDE, SHIFT = 512, 384, 16
SLOT_PIECE = 16


def dot(a, b, contract=((1,), (0,)), precision=None):
    return lax.dot_general(a, b, (contract, ((), ())), precision=precision, preferred_element_type=f32)


def gram_of(rows):
    return dot(rows, rows, ((0,), (0,)), highest)


def diagonal_mask():
    return lax.broadcasted_iota(jnp.int32, (R, R), 0) == lax.broadcasted_iota(jnp.int32, (R, R), 1)


def regularize(matrix):
    eye = diagonal_mask()
    mean = jnp.sum(jnp.where(eye, matrix, 0.0)) / R
    return matrix + jnp.where(eye, ridge_scale * mean, 0.0)


def inverse(matrix):
    lane = lax.broadcasted_iota(jnp.int32, (8, R), 1)
    sub = lax.broadcasted_iota(jnp.int32, (8, R), 0)
    lane_rest = lax.broadcasted_iota(jnp.int32, (R - 8, R), 1)

    def step(_, matrix):
        top, rest = matrix[0:8], matrix[8:]
        rows = [jnp.broadcast_to(top[i : i + 1, :], (8, R)) for i in range(8)]
        a = {(i, j): jnp.broadcast_to(rows[i][:, j : j + 1], (8, R)) for i in range(8) for j in range(i, 8)}
        rows = [jnp.where(lane == i, 1.0, jnp.where(lane < 8, 0.0, rows[i])) for i in range(8)]
        lower, scale = {}, []
        for t in range(8):
            scale.append(1.0 / a[t, t])
            for s in range(t + 1, 8):
                lower[s, t] = a[t, s] * scale[t]
            for s in range(t + 1, 8):
                for u in range(s, 8):
                    a[s, u] = a[s, u] - lower[s, t] * a[t, u]
                rows[s] = rows[s] - lower[s, t] * rows[t]
        rows = [rows[t] * scale[t] for t in range(8)]
        for t in range(7, -1, -1):
            for s in range(t):
                rows[s] = rows[s] - lower[t, s] * rows[t]
        new_top = rows[7]
        for i in range(7):
            new_top = jnp.where(sub == i, rows[i], new_top)
        base = jnp.where(lane_rest < 8, 0.0, rest)
        for i in range(8):
            base = base - rest[:, i : i + 1] * rows[i][0:1, :]
        return pltpu.roll(jnp.concatenate([base, new_top], axis=0), R - 8, 1)

    return lax.fori_loop(0, R // 8, step, matrix)


def split(value):
    high = value.astype(bf16)
    return high, (value - high.astype(f32)).astype(bf16)


class Exchange:
    def __init__(self, refs, count, me, device, source=None):
        self.buffer, self.send_sem, self.recv_sem = refs
        self.count, self.me, self.device, self.source = count, me, device, source

    def copy(self, k, slot):
        peer = lax.rem(self.me + k, self.count)
        source = self.buffer.at[self.me] if self.source is None else self.source.at[peer]
        return pltpu.make_async_remote_copy(
            src_ref=source,
            dst_ref=self.buffer.at[self.me if slot is None else peer],
            send_sem=self.send_sem.at[k],
            recv_sem=self.recv_sem.at[self.me if slot is None else peer],
            device_id=self.device(peer),
            device_id_type=MESH,
        )

    def each(self, act):
        def step(i, carry):
            act(lax.rem(i + self.count // 2 - 1, self.count - 1) + 1)
            return carry

        lax.fori_loop(0, self.count - 1, step, 0)

    def start(self):
        self.each(lambda k: self.copy(k, None).start())

    def wait_recv(self):
        self.each(lambda k: self.copy(k, "peer").wait_recv())

    def wait_send(self):
        self.each(lambda k: self.copy(k, None).wait_send())

    def total(self):
        total = self.buffer[0]
        for i in range(1, self.count):
            total = total + self.buffer[i]
        return total


def body(
    sensor_count, slot_count,
    traffic, slot_ref, day_ref, sensor_out, slot_out, day_out,
    t_all, t_high, t_low, w_cat, load_sem,
    win_sib, win_own, sib_recv, sib_ssem, sib_rsem, x_send, x_recv, x_ssem, x_rsem,
    gathered, gat_ssem, gat_rsem, fwd_ssem, fwd_rsem,
    c_wide, c_low,
    gram_part, gx_buf, gx_s, gx_r, gy_buf, gy_s, gy_r, gz_buf, gz_s, gz_r, ga_buf, ga_s, ga_r,
    slot_part, s8_buf, s8_s, s8_r, sz_buf, sz_s, sz_r, sa_buf, sa_s, sa_r, sx_buf, sx_s, sx_r,
    dy_buf, dy_s, dy_r, dz_buf, dz_s, dz_r,
):
    days, slots, sensors = traffic.shape
    rows = days * slots
    padded = t_all.shape[0]
    own = sensors // GROUP
    sensor_index = lax.axis_index("sensor")
    slot_index = lax.axis_index("slot")
    day_index = lax.axis_index("day")
    z, y = sensor_index // NY, lax.rem(sensor_index, NY)
    core = lax.rem(slot_index, 2)
    x_hi = slot_index // 2
    x = x_hi * 2 + day_index

    def device(z, y, x, core):
        return (z * NY + y, (x // 2) * 2 + core, lax.rem(x, 2))

    def chunk_of(x, core):
        return ((x // 2) * 2 + core) * 2 + lax.rem(x, 2)

    def group_device(index):
        return (sensor_index, index // 2, lax.rem(index, 2))

    me = chunk_of(x, core)

    barrier = pltpu.get_barrier_semaphore()

    def greet(target):
        pl.semaphore_signal(barrier, inc=1, device_id=target, device_id_type=MESH)

    def greet_group(k, carry):
        greet(group_device(lax.rem(me + k, GROUP)))
        return carry

    def greet_z(k, carry):
        greet(device(lax.rem(z + k, NZ), y, x, core))
        return carry

    def greet_y(k, carry):
        other = lax.rem(y + k, NY)
        for cx, cc in ((0, 0), (0, 1), (2, 0), (2, 1), (None, 0)):
            if cx is None:
                greet(device(z, other, x_hi * 2 + 1 - day_index, core))
            else:
                greet(device(z, other, lax.rem(x + cx, NX), lax.rem(core + cc, 2)))
        return carry

    lax.fori_loop(1, GROUP, greet_group, 0)
    lax.fori_loop(1, NZ, greet_z, 0)
    lax.fori_loop(1, NY, greet_y, 0)

    loads = []
    for k in range(days):
        copy = pltpu.make_async_copy(traffic.at[k], t_all.at[pl.ds(k * slots, slots)], load_sem.at[k])
        copy.start()
        loads.append(copy)

    slot_local = slot_ref[pl.ds(pl.multiple_of(slot_index * slots, 8), slots), :]
    khatri = [slot_local * day_ref[pl.ds(day_index * days + k, 1), :] for k in range(days)]
    khatri = jnp.concatenate(khatri + [jnp.zeros((padded - rows, R), f32)], axis=0)
    w_high, w_low = split(khatri)
    w_cat[:, 0:R] = w_high
    w_cat[:, R:] = w_low
    t_all[pl.ds(rows, padded - rows), :] = jnp.zeros((padded - rows, sensors), f32)
    gathered[...] = jnp.zeros_like(gathered)
    c_wide[...] = jnp.zeros_like(c_wide)
    c_low[...] = jnp.zeros_like(c_low)
    for copy in loads:
        copy.wait()

    def convert(i, carry):
        lanes = pl.ds(pl.multiple_of(i * R, R), R)
        t_high[:, lanes], t_low[:, lanes] = split(t_all[:, lanes])
        return carry

    lax.fori_loop(0, sensors // R, convert, 0)

    def window_of(chunk):
        return pl.ds(pl.multiple_of(chunk * STRIDE, R), WINDOW)

    def rows_of(chunk):
        return pl.ds(pl.multiple_of(chunk * SHIFT, SHIFT), own)

    def first_product(chunk, target):
        lanes = window_of(chunk)
        wide = dot(t_high[:, lanes], w_cat[...], ((0,), (0,)))
        low = dot(t_low[:, lanes], w_cat[:, 0:R], ((0,), (0,)))
        target[...] = wide[:, 0:R] + wide[:, R:] + low

    def target_x(j):
        return lax.rem(x + jnp.where(j == 0, 2, jnp.where(j == 1, 1, jnp.where(j == 2, 3, 0))), NX)

    def sibling_copy(j):
        chunk = chunk_of(target_x(j), 1 - core)
        return pltpu.make_async_remote_copy(
            src_ref=win_sib.at[j].at[rows_of(chunk)], dst_ref=sib_recv.at[j],
            send_sem=sib_ssem.at[j], recv_sem=sib_rsem.at[j],
            device_id=device(z, y, x, 1 - core), device_id_type=MESH,
        )

    def x_copy(j):
        return pltpu.make_async_remote_copy(
            src_ref=x_send.at[j], dst_ref=x_recv.at[j],
            send_sem=x_ssem.at[j], recv_sem=x_rsem.at[j],
            device_id=device(z, y, target_x(j), core), device_id_type=MESH,
        )

    def scatter_step(j, carry):
        @pl.when(j < NX)
        def _():
            first_product(chunk_of(target_x(j), 1 - core), win_sib.at[j])

            @pl.when(j == 0)
            def _():
                pl.semaphore_wait(barrier, 7 + (NZ - 1) + 5 * (NY - 1))

            sibling_copy(j).start()
            first_product(chunk_of(target_x(j), core), win_own.at[j])

        @pl.when(j > 0)
        def _():
            sibling_copy(j - 1).wait_recv()
            x_send[j - 1] = win_own[j - 1, rows_of(chunk_of(target_x(j - 1), core)), :] + sib_recv[j - 1]

            @pl.when(j < NX)
            def _():
                x_copy(j - 1).start()

        return carry

    lax.fori_loop(0, NX + 1, scatter_step, 0)

    gram_day = gram_of(day_ref[...])
    inv_sensor = inverse(regularize(gram_of(slot_ref[...]) * gram_day))

    right_side = x_send[NX - 1]
    for j in range(NX - 1):
        x_copy(j).wait_recv()
        right_side = right_side + x_recv[j]
    sensor_raw = dot(right_side, inv_sensor, precision=highest)
    gathered[me, rows_of(me), :] = sensor_raw

    def device_y(p):
        return device(z, p, x, core)

    def device_z(p):
        return device(p, y, x, core)

    gram = gram_of(sensor_raw)
    for i in range(GROUP):
        gram_part[i] = gram[16 * i : 16 * i + 16]
    gx = Exchange((gx_buf, gx_s, gx_r), GROUP, me, group_device, gram_part)
    gy = Exchange((gy_buf, gy_s, gy_r), NY, y, device_y)
    gz = Exchange((gz_buf, gz_s, gz_r), NZ, z, device_z)
    ga = Exchange((ga_buf, ga_s, ga_r), GROUP, me, group_device)
    gx.start()
    gx_buf[me] = gram_part[me]

    def gather_copy(j, sender=False):
        chunk = me if sender else chunk_of(source_x(j), core)
        place = gathered.at[chunk].at[rows_of(chunk)]
        return pltpu.make_async_remote_copy(
            src_ref=place, dst_ref=place, send_sem=gat_ssem.at[j], recv_sem=gat_rsem.at[j],
            device_id=device(z, y, target_x(j), core), device_id_type=MESH,
        )

    def source_x(j):
        return lax.rem(x + jnp.where(j == 0, 2, jnp.where(j == 1, 3, jnp.where(j == 2, 1, 0))), NX)

    def forward_copy(j, sender=False):
        chunk = chunk_of(source_x(j), core if sender else 1 - core)
        place = gathered.at[chunk].at[rows_of(chunk)]
        return pltpu.make_async_remote_copy(
            src_ref=place, dst_ref=place, send_sem=fwd_ssem.at[j], recv_sem=fwd_rsem.at[j],
            device_id=device(z, y, x, 1 - core), device_id_type=MESH,
        )

    for j in (1, 2, 0):
        gather_copy(j, True).start()
    forward_copy(3, True).start()

    def second_product(chunk):
        lanes = window_of(chunk)
        high, low = split(gathered[chunk])
        c_wide[...] += dot(t_high[:, lanes], jnp.concatenate([high, low], axis=1))
        c_low[...] += dot(t_low[:, lanes], high)

    def gather_step(i, carry):
        j = 3 - i
        j = jnp.where(i == 0, 3, jnp.where(i == 1, 1, jnp.where(i == 2, 2, 0)))

        @pl.when(i > 0)
        def _():
            gather_copy(j).wait_recv()
            forward_copy(j, True).start()

        second_product(chunk_of(source_x(j), core))
        forward_copy(j).wait_recv()
        second_product(chunk_of(source_x(j), 1 - core))

        @pl.when(i == 1)
        def _():
            gx.wait_recv()
            gy_buf[y] = gx.total()
            gy.start()

        @pl.when(i == 2)
        def _():
            gy.wait_recv()
            gz_buf[z] = gy.total()
            gz.start()

        return carry

    lax.fori_loop(0, NX, gather_step, 0)

    contracted = c_wide[:, 0:R] + c_wide[:, R:] + c_low[...]
    contracted = [contracted[k * slots : (k + 1) * slots] for k in range(days)]
    part = contracted[0] * day_ref[pl.ds(day_index * days, 1), :]
    for k in range(1, days):
        part = part + contracted[k] * day_ref[pl.ds(day_index * days + k, 1), :]
    piece = slots // 8
    for i in range(8):
        slot_part[i, 0:piece] = part[i * piece : (i + 1) * piece]
        slot_part[i, piece:] = jnp.zeros((SLOT_PIECE - piece, R), f32)

    def device_8(p):
        return device(z, p // 2, x_hi * 2 + lax.rem(p, 2), core)

    def device_slot(p):
        return (sensor_index, p, day_index)

    me_8 = y * 2 + day_index
    s8 = Exchange((s8_buf, s8_s, s8_r), 8, me_8, device_8, slot_part)
    sz = Exchange((sz_buf, sz_s, sz_r), NZ, z, device_z)
    sa = Exchange((sa_buf, sa_s, sa_r), 8, me_8, device_8)
    sx = Exchange((sx_buf, sx_s, sx_r), 4, slot_index, device_slot)
    s8.start()
    s8_buf[me_8] = slot_part[me_8]
    s8.wait_recv()
    sz_buf[z] = s8.total()
    sz.start()

    gz.wait_recv()
    ga_buf[me] = gz.total()
    ga.start()
    ga.wait_recv()
    gram = jnp.concatenate([ga_buf[i] for i in range(GROUP)], axis=0)

    def norms_of(gram, count):
        square = jnp.where(diagonal_mask(), gram, 0.0)
        row = jnp.sqrt(jnp.sum(square, axis=0, keepdims=True) / count + epsilon)
        column = jnp.sqrt(jnp.sum(square, axis=1, keepdims=True) / count + epsilon)
        return row, gram / (column * row)

    sensor_norms, gram_sensor = norms_of(gram, sensor_count)
    sensor_out[...] = gathered[me, rows_of(me), :] / sensor_norms
    inv_slot = inverse(regularize(gram_sensor * gram_day))

    sz.wait_recv()
    sa_buf[me_8] = sz.total()
    sa.start()
    sa.wait_recv()
    slot_rhs = jnp.concatenate([sa_buf[i][0:piece] for i in range(8)], axis=0) / sensor_norms
    slot_raw = dot(slot_rhs, inv_slot, precision=highest)
    sx_buf[slot_index] = slot_raw
    sx.start()
    sx.wait_recv()
    gram = gram_of(sx_buf[0])
    for i in range(1, 4):
        gram = gram + gram_of(sx_buf[i])
    slot_norms, gram_slot_new = norms_of(gram, slot_count)
    slot_new = slot_raw / slot_norms
    slot_out[...] = slot_new

    weight = slot_new / sensor_norms
    day_part = [jnp.sum(c * weight, axis=0, keepdims=True) for c in contracted]
    day_part = jnp.concatenate(day_part + [jnp.zeros((8 - days, R), f32)], axis=0)

    def device_16(p):
        return (z * NY + p // 4, lax.rem(p, 4), day_index)

    me_16 = y * 4 + slot_index
    dy = Exchange((dy_buf, dy_s, dy_r), 16, me_16, device_16)
    dz = Exchange((dz_buf, dz_s, dz_r), NZ, z, device_z)
    dy_buf[me_16] = day_part
    dy.start()
    inv_day = inverse(regularize(gram_sensor * gram_slot_new))
    dy.wait_recv()
    dz_buf[z] = dy.total()
    dz.start()
    dz.wait_recv()
    day_new = dot(dz.total(), inv_day, precision=highest)
    day_out[...] = day_new[0:days]

    def drain(j, carry):
        sibling_copy(j).wait_send()
        forward_copy(j, True).wait_send()

        @pl.when(j < NX - 1)
        def _():
            x_copy(j).wait_send()
            gather_copy(j, True).wait_send()

        return carry

    lax.fori_loop(0, NX, drain, 0)
    for exchange in (gx, gy, gz, ga, s8, sz, sa, sx, dy, dz):
        exchange.wait_send()


def on_device(traffic, slot_factor, day_factor):
    days, slots, sensors = traffic.shape
    slot_count = slot_factor.shape[0]
    sensor_count = sensors * lax.axis_size("sensor")
    own = sensors // GROUP
    padded = (days * slots + 15) // 16 * 16

    def exchange_scratch(count, *block):
        return [
            pltpu.VMEM((count, *block), f32),
            pltpu.SemaphoreType.DMA((count,)),
            pltpu.SemaphoreType.DMA((count,)),
        ]

    dma = pltpu.SemaphoreType.DMA
    scratch = [
        pltpu.VMEM((padded, sensors), f32),
        pltpu.VMEM((padded, sensors), bf16),
        pltpu.VMEM((padded, sensors), bf16),
        pltpu.VMEM((padded, 2 * R), bf16),
        dma((days,)),
        pltpu.VMEM((NX, WINDOW, R), f32),
        pltpu.VMEM((NX, WINDOW, R), f32),
        *exchange_scratch(NX, own, R),
        pltpu.VMEM((NX, own, R), f32),
        *exchange_scratch(NX - 1, own, R),
        pltpu.VMEM((GROUP, WINDOW, R), f32),
        dma((NX - 1,)), dma((NX - 1,)), dma((NX,)), dma((NX,)),
        pltpu.VMEM((padded, 2 * R), f32),
        pltpu.VMEM((padded, R), f32),
        pltpu.VMEM((GROUP, 16, R), f32),
        *exchange_scratch(GROUP, 16, R),
        *exchange_scratch(NY, 16, R),
        *exchange_scratch(NZ, 16, R),
        *exchange_scratch(GROUP, 16, R),
        pltpu.VMEM((8, SLOT_PIECE, R), f32),
        *exchange_scratch(8, SLOT_PIECE, R),
        *exchange_scratch(NZ, SLOT_PIECE, R),
        *exchange_scratch(8, SLOT_PIECE, R),
        *exchange_scratch(4, slots, R),
        *exchange_scratch(16, 8, R),
        *exchange_scratch(NZ, 8, R),
    ]
    vmem = pl.BlockSpec(memory_space=pltpu.VMEM)

    def kernel(*refs):
        body(sensor_count, slot_count, *refs)

    return pl.pallas_call(
        kernel,
        out_shape=(
            jax.ShapeDtypeStruct((own, R), f32),
            jax.ShapeDtypeStruct((slots, R), f32),
            jax.ShapeDtypeStruct((days, R), f32),
        ),
        in_specs=[pl.BlockSpec(memory_space=pl.ANY), vmem, vmem],
        out_specs=(vmem, vmem, vmem),
        scratch_shapes=scratch,
        compiler_params=pltpu.CompilerParams(
            collective_id=0, has_side_effects=True, vmem_limit_bytes=48 * 1024 * 1024
        ),
    )(traffic, slot_factor, day_factor)


def solution(mesh):
    in_specs = (P("day", "slot", "sensor"), P(), P())
    out_specs = (P(("sensor", "slot", "day"), None), P("slot", None), P("day", None))
    return jax.shard_map(
        on_device, mesh=mesh, in_specs=in_specs, out_specs=out_specs, check_vma=False
    )
```

time: 1770 us -> 99.9 us (0.06)
  blocking collectives: 1140 us -> 0 us
  waiting for transfers between devices: 472 us -> 0 us
  Pallas kernels: 0 us -> 93.3 us
  other arithmetic: 71.7 us -> 0 us
  matrix products: 45.7 us -> 0 us
    psum x2 -> x0, blocking collectives: 1140 us -> none  [the longest x1 646 us: on_device(): day_rhs = lax.psum(day_part, ('sensor', 'slot'))]
    psum x3 -> x0, waiting for transfers between devices: 472 us -> none  [the longest x1 249 us: on_device(): raw_gram = lax.psum(gram_of(block_raw), 'sensor')]
    pallas_call x0 -> x1, Pallas kernels: none -> 93.3 us  [on_device(): pl.pallas_call(kernel, out_shape=(jax.ShapeDtypeStruct((own, R), f32), ja...]
    another operation x15 -> x0, other arithmetic: 68.6 us -> none  [the longest x9 37.2 us: solve_rows(): lower_factor = jnp.linalg.cholesky(normal_matrix)]
    dot_general x7 -> x0, matrix products: 38.5 us -> none  [the longest x1 17.7 us: on_device(): jnp.einsum('kir,kr->ir', partial_value, day_local, precision=highest)]
  transfers between devices with their start and end apart: 3 -> 0, of which waited for: 3 -> 0; matrix products, arithmetic and copies ran while one was open for 2% -> 0% of each run, Pallas kernels for 0% -> 0%
where the time goes in v1:
time: 99.9 us; the launch traced here: 99.7 us
  Pallas kernels  93.3 us (93%)
  local copies, waits for them, and re-layouts  5.79 us (6%)
    pallas_call x1, Pallas kernels, on_device(): pl.pallas_call(kernel, out_shape=(jax.ShapeDtypeStruct((own, R), f32), ja...  93.3 us
    unnamed x9, local copies, waits for them, and re-layouts  5.79 us

profile of v1, /device:TPU:1, one launch (start us, length us, event | category | flops | bytes accessed | tf_op | source)
XLA Modules:
  0.0 99.7 jit_solution(12328295097126536053)
XLA Ops:
  0.6 0.0 copy-start
  0.6 2.3 %copy-done = f32[5,72,3200]{2,1,0:T(8,128)S(1)} copy-done((f32[5,72,3200]{2,1,0:T(8,128)S(1)}, f32[5,72,3200]{2,1,0:T(8,128)}, u32[]{:S(2)}) %copy-start) | copy-done | bytes 4608024
  2.9 0.0 copy-start.1
  2.9 0.9 copy-done.1
  3.8 0.0 copy-start.2
  3.8 0.7 copy-done.2
  4.5 93.3 %shard_map.58 = (f32[400,128]{1,0:T(8,128)S(1)}, f32[72,128]{1,0:T(8,128)S(1)}, f32[5,128]{1,0:T(8,128)S(1)}) custom-call(f32[5,72,3200]{2,1,0:T(8,128)S(1)} %copy-done, f32[288,128]{1,0:T(8,128)S(1)} %copy-done.1, f32[10,128]{1,0:T(8,128)S(1)} %copy-done.2), custom_call_target="tpu_custom_call" | custom-call | tf_op jit(solution)/shard_map/pallas_call | solution.py:487
  97.8 0.7 copy.9
  98.5 0.6 copy.10
  99.1 0.6 copy.11
Async XLA Ops:
  0.6 2.3 %copy-start = (f32[5,72,3200]{2,1,0:T(8,128)S(1)}, f32[5,72,3200]{2,1,0:T(8,128)}, u32[]{:S(2)}) copy-start(f32[5,72,3200]{2,1,0:T(8,128)} %refs_0_.1) | copy-start | bytes 13824004
  2.9 0.9 copy-start.1
  3.8 0.7 copy-start.2

commit v2 on v1

v2 whole, which is shorter than its diff:
```python
import jax
import jax.numpy as jnp
from jax import lax
from jax.experimental import pallas as pl
from jax.experimental.pallas import tpu as pltpu
from jax.sharding import PartitionSpec as P

MESH = pl.DeviceIdType.MESH
highest = lax.Precision.HIGHEST
f32 = jnp.float32
bf16 = jnp.bfloat16
ridge_scale = 0.001
epsilon = 1e-05

R = 128
NX, NY, NZ = 4, 4, 16
GROUP = 8
WINDOW, STRIDE, SHIFT = 512, 384, 16


def dot(a, b, contract=((1,), (0,)), precision=None):
    return lax.dot_general(a, b, (contract, ((), ())), precision=precision, preferred_element_type=f32)


def gram_of(rows):
    return dot(rows, rows, ((0,), (0,)), highest)


def diagonal_mask():
    return lax.broadcasted_iota(jnp.int32, (R, R), 0) == lax.broadcasted_iota(jnp.int32, (R, R), 1)


def regularize(matrix):
    eye = diagonal_mask()
    mean = jnp.sum(jnp.where(eye, matrix, 0.0)) / R
    return matrix + jnp.where(eye, ridge_scale * mean, 0.0)


def inverse(matrix):
    lane = lax.broadcasted_iota(jnp.int32, (8, R), 1)
    sub = lax.broadcasted_iota(jnp.int32, (8, R), 0)
    lane_rest = lax.broadcasted_iota(jnp.int32, (R - 8, R), 1)

    def step(_, matrix):
        top, rest = matrix[0:8], matrix[8:]
        rows = [jnp.broadcast_to(top[i : i + 1, :], (8, R)) for i in range(8)]
        a = {(i, j): jnp.broadcast_to(rows[i][:, j : j + 1], (8, R)) for i in range(8) for j in range(i, 8)}
        rows = [jnp.where(lane == i, 1.0, jnp.where(lane < 8, 0.0, rows[i])) for i in range(8)]
        lower, scale = {}, []
        for t in range(8):
            scale.append(1.0 / a[t, t])
            for s in range(t + 1, 8):
                lower[s, t] = a[t, s] * scale[t]
            for s in range(t + 1, 8):
                for u in range(s, 8):
                    a[s, u] = a[s, u] - lower[s, t] * a[t, u]
                rows[s] = rows[s] - lower[s, t] * rows[t]
        rows = [rows[t] * scale[t] for t in range(8)]
        for t in range(7, -1, -1):
            for s in range(t):
                rows[s] = rows[s] - lower[t, s] * rows[t]
        new_top = rows[7]
        for i in range(7):
            new_top = jnp.where(sub == i, rows[i], new_top)
        base = jnp.where(lane_rest < 8, 0.0, rest)
        for i in range(8):
            base = base - rest[:, i : i + 1] * rows[i][0:1, :]
        return pltpu.roll(jnp.concatenate([base, new_top], axis=0), R - 8, 1)

    return lax.fori_loop(0, R // 8, step, matrix)


def split(value):
    high = value.astype(bf16)
    return high, (value - high.astype(f32)).astype(bf16)


class Exchange:
    def __init__(self, refs, count, me, device, source=None):
        self.buffer, self.send_sem, self.recv_sem = refs
        self.count, self.me, self.device, self.source = count, me, device, source

    def copy(self, k, slot):
        peer = lax.rem(self.me + k, self.count)
        source = self.buffer.at[self.me] if self.source is None else self.source.at[peer]
        return pltpu.make_async_remote_copy(
            src_ref=source,
            dst_ref=self.buffer.at[self.me if slot is None else peer],
            send_sem=self.send_sem.at[k],
            recv_sem=self.recv_sem.at[self.me if slot is None else peer],
            device_id=self.device(peer),
            device_id_type=MESH,
        )

    def each(self, act):
        middle = self.count // 2

        def step(i, carry):
            act(middle + jnp.where(lax.rem(i, 2) == 1, (i + 1) // 2, -(i // 2)))
            return carry

        lax.fori_loop(0, self.count - 1, step, 0)

    def start(self):
        self.each(lambda k: self.copy(k, None).start())

    def wait_recv(self):
        self.each(lambda k: self.copy(k, "peer").wait_recv())

    def wait_send(self):
        self.each(lambda k: self.copy(k, None).wait_send())

    def total(self):
        total = self.buffer[0]
        for i in range(1, self.count):
            total = total + self.buffer[i]
        return total


def body(
    sensor_count, slot_count,
    traffic, slot_in, day_in, sensor_out, slot_out, day_out,
    slot_ref, day_ref, t_win, t_high, t_low, w_cat, factor_sem, load_sem,
    win_sib, win_own, sib_recv, sib_ssem, sib_rsem, x_send, x_recv, x_ssem, x_rsem,
    gathered, gat_ssem, gat_rsem, fwd_ssem, fwd_rsem,
    c_wide, c_low,
    gram_part, gram_rows, gx_buf, gx_s, gx_r, gy_buf, gy_s, gy_r, gz_buf, gz_s, gz_r, ga_buf, ga_s, ga_r,
    slot_part, s8_buf, s8_s, s8_r, sz_buf, sz_s, sz_r, sa_buf, sa_s, sa_r, slot_all,
    con_part, con_rows, cy_buf, cy_s, cy_r, cz_buf, cz_s, cz_r, ca_buf, ca_s, ca_r, weights,
    dy_buf, dy_s, dy_r,
):
    days, slots, sensors = traffic.shape
    rows = days * slots
    padded = w_cat.shape[0]
    strips = NZ // days
    strip = slots // NY // strips
    own = sensors // GROUP
    sensor_index = lax.axis_index("sensor")
    slot_index = lax.axis_index("slot")
    day_index = lax.axis_index("day")
    z, y = sensor_index // NY, lax.rem(sensor_index, NY)
    core = lax.rem(slot_index, 2)
    x_hi = slot_index // 2
    x = x_hi * 2 + day_index

    def device(z, y, x, core):
        return (z * NY + y, (x // 2) * 2 + core, lax.rem(x, 2))

    def chunk_of(x, core):
        return ((x // 2) * 2 + core) * 2 + lax.rem(x, 2)

    def group_device(index):
        return (sensor_index, index // 2, lax.rem(index, 2))

    me = chunk_of(x, core)

    barrier = pltpu.get_barrier_semaphore()

    def greet(target):
        pl.semaphore_signal(barrier, inc=1, device_id=target, device_id_type=MESH)

    def greet_group(k, carry):
        greet(group_device(lax.rem(me + k, GROUP)))
        return carry

    def greet_z(k, carry):
        greet(device(lax.rem(z + k, NZ), y, x, core))
        return carry

    def greet_y(k, carry):
        other = lax.rem(y + k, NY)
        for cx, cc in ((0, 0), (0, 1), (2, 0), (2, 1), (None, 0)):
            if cx is None:
                greet(device(z, other, x_hi * 2 + 1 - day_index, core))
            else:
                greet(device(z, other, lax.rem(x + cx, NX), lax.rem(core + cc, 2)))
        return carry

    lax.fori_loop(1, GROUP, greet_group, 0)
    lax.fori_loop(1, NZ, greet_z, 0)
    lax.fori_loop(1, NY, greet_y, 0)

    factor_loads = [
        pltpu.make_async_copy(slot_in, slot_ref, factor_sem.at[0]),
        pltpu.make_async_copy(day_in, day_ref, factor_sem.at[1]),
    ]
    for copy in factor_loads:
        copy.start()

    def target_x(j):
        return lax.rem(x + jnp.where(j == 0, 2, jnp.where(j == 1, 1, jnp.where(j == 2, 3, 0))), NX)

    def load_copy(chunk):
        lanes = pl.ds(pl.multiple_of(chunk * STRIDE, R), WINDOW)
        return pltpu.make_async_copy(traffic.at[:, :, lanes], t_win.at[chunk], load_sem.at[chunk])

    def load_step(j, carry):
        load_copy(chunk_of(target_x(j), 1 - core)).start()
        load_copy(chunk_of(target_x(j), core)).start()
        return carry

    lax.fori_loop(0, NX, load_step, 0)

    for c in range(GROUP):
        if c:
            gathered[c, 0 : SHIFT * c] = jnp.zeros((SHIFT * c, R), f32)
        if SHIFT * c + own < WINDOW:
            gathered[c, SHIFT * c + own :] = jnp.zeros((WINDOW - own - SHIFT * c, R), f32)
    c_wide[...] = jnp.zeros_like(c_wide)
    c_low[...] = jnp.zeros_like(c_low)
    for copy in factor_loads:
        copy.wait()

    slot_local = slot_ref[pl.ds(pl.multiple_of(slot_index * slots, 8), slots), :]
    khatri = [slot_local * day_ref[pl.ds(day_index * days + k, 1), :] for k in range(days)]
    khatri = jnp.concatenate(khatri + [jnp.zeros((padded - rows, R), f32)], axis=0)
    w_high, w_low = split(khatri)
    w_cat[:, 0:R] = w_high
    w_cat[:, R:] = w_low

    half = own // 2

    def rows_of(chunk):
        return pl.ds(pl.multiple_of(chunk * SHIFT, SHIFT), own)

    def half_rows_of(chunk, h):
        return pl.ds(pl.multiple_of(chunk * SHIFT + h * half, 8), half)

    def first_product(chunk, target):
        load_copy(chunk).wait()
        block = [t_win[chunk, k] for k in range(days)] + [jnp.zeros((padded - rows, WINDOW), f32)]
        high, low = split(jnp.concatenate(block, axis=0))
        t_high[chunk] = high
        t_low[chunk] = low
        wide = dot(high, w_cat[...], ((0,), (0,)))
        target[...] = wide[:, 0:R] + wide[:, R:] + dot(low, w_cat[:, 0:R], ((0,), (0,)))

    def sibling_copy(j):
        chunk = chunk_of(target_x(j), 1 - core)
        return pltpu.make_async_remote_copy(
            src_ref=win_sib.at[j].at[rows_of(chunk)], dst_ref=sib_recv.at[j],
            send_sem=sib_ssem.at[j], recv_sem=sib_rsem.at[j],
            device_id=device(z, y, x, 1 - core), device_id_type=MESH,
        )

    def x_copy(j, h):
        rows_h = pl.ds(pl.multiple_of(h * half, 8), half)
        return pltpu.make_async_remote_copy(
            src_ref=x_send.at[j].at[rows_h], dst_ref=x_recv.at[j].at[rows_h],
            send_sem=x_ssem.at[j, h], recv_sem=x_rsem.at[j, h],
            device_id=device(z, y, target_x(j), core), device_id_type=MESH,
        )

    def scatter_step(j, carry):
        @pl.when(j < NX)
        def _():
            first_product(chunk_of(target_x(j), 1 - core), win_sib.at[j])
            first_product(chunk_of(target_x(j), core), win_own.at[j])

            @pl.when(j == 0)
            def _():
                pl.semaphore_wait(barrier, 7 + (NZ - 1) + 5 * (NY - 1))

            sibling_copy(j).start()

        @pl.when(j > 0)
        def _():
            sibling_copy(j - 1).wait_recv()
            x_send[j - 1] = win_own[j - 1, rows_of(chunk_of(target_x(j - 1), core)), :] + sib_recv[j - 1]

            @pl.when(j < NX)
            def _():
                x_copy(j - 1, 0).start()

        return carry

    lax.fori_loop(0, NX + 1, scatter_step, 0)
    for j in range(NX - 1):
        x_copy(j, 1).start()

    gram_day = gram_of(day_ref[...])
    inv_sensor = inverse(regularize(gram_of(slot_ref[...]) * gram_day))

    def own_half(h):
        total = x_send[NX - 1, h * half : (h + 1) * half]
        for j in range(NX - 1):
            x_copy(j, h).wait_recv()
            total = total + x_recv[j, h * half : (h + 1) * half]
        sensor_raw = dot(total, inv_sensor, precision=highest)
        gathered[me, half_rows_of(me, h), :] = sensor_raw
        return gram_of(sensor_raw)

    def device_y(p):
        return device(z, p, x, core)

    def device_z(p):
        return device(p, y, x, core)

    def device_32(p):
        return (z * NY + p // 8, lax.rem(p // 2, 4), lax.rem(p, 2))

    me_32 = y * 8 + me
    gx = Exchange((gx_buf, gx_s, gx_r), GROUP, me, group_device, gram_part)
    gy = Exchange((gy_buf, gy_s, gy_r), NY, y, device_y, gram_rows)
    gz = Exchange((gz_buf, gz_s, gz_r), NZ, z, device_z)
    ga = Exchange((ga_buf, ga_s, ga_r), 32, me_32, device_32)

    def source_x(j):
        return lax.rem(x + jnp.where(j == 0, 2, jnp.where(j == 1, 3, jnp.where(j == 2, 1, 0))), NX)

    def gather_copy(j, h, sender=False):
        chunk = me if sender else chunk_of(source_x(j), core)
        place = gathered.at[chunk].at[half_rows_of(chunk, h)]
        return pltpu.make_async_remote_copy(
            src_ref=place, dst_ref=place, send_sem=gat_ssem.at[j, h], recv_sem=gat_rsem.at[j, h],
            device_id=device(z, y, target_x(j), core), device_id_type=MESH,
        )

    def forward_copy(j, h, sender=False):
        chunk = chunk_of(source_x(j), core if sender else 1 - core)
        place = gathered.at[chunk].at[half_rows_of(chunk, h)]
        return pltpu.make_async_remote_copy(
            src_ref=place, dst_ref=place, send_sem=fwd_ssem.at[j, h], recv_sem=fwd_rsem.at[j, h],
            device_id=device(z, y, x, 1 - core), device_id_type=MESH,
        )

    def gather_start(h):
        for j in (1, 2, 0):
            gather_copy(j, h, True).start()
        forward_copy(3, h, True).start()

    gram = own_half(0)
    gather_start(0)
    gram = gram + own_half(1)
    for i in range(GROUP):
        gram_part[i] = gram[16 * i : 16 * i + 16]
    gx.start()
    gx_buf[me] = gram_part[me]
    gather_start(1)

    def second_product(chunk):
        high, low = split(gathered[chunk])
        c_wide[...] += dot(t_high[chunk], jnp.concatenate([high, low], axis=1))
        c_low[...] += dot(t_low[chunk], high)

    def own_core(j):
        second_product(chunk_of(source_x(j), core))

    def other_core(j):
        forward_copy(j, 0).wait_recv()
        forward_copy(j, 1).wait_recv()
        second_product(chunk_of(source_x(j), 1 - core))

    def pass_on(j, h):
        gather_copy(j, h).wait_recv()
        forward_copy(j, h, True).start()

    def gather_step(i, carry):
        @pl.when(i == 0)
        def _():
            own_core(3)
            other_core(3)
            pass_on(1, 0)
            pass_on(2, 0)
            pass_on(0, 0)
            gx.wait_recv()
            gram = gx.total()
            for i in range(NY):
                gram_rows[i] = gram[4 * i : 4 * i + 4]
            gy.start()
            gy_buf[y] = gram_rows[y]
            pass_on(1, 1)
            pass_on(2, 1)

        @pl.when(i == 3)
        def _():
            pass_on(0, 1)

        j = jnp.where(i == 0, 1, jnp.where(i == 1, 2, 0))

        @pl.when(i != 2)
        def _():
            own_core(j)

        @pl.when(i == 2)
        def _():
            gy.wait_recv()
            gz_buf[z] = gy.total()
            gz.start()

        @pl.when(i >= 2)
        def _():
            other_core(jnp.where(i == 2, 1, 0))

        @pl.when(i == 2)
        def _():
            other_core(2)

        return carry

    lax.fori_loop(0, NX, gather_step, 0)

    contracted = c_wide[:, 0:R] + c_wide[:, R:] + c_low[...]
    contracted = [contracted[k * slots : (k + 1) * slots] for k in range(days)]
    part = contracted[0] * day_ref[pl.ds(day_index * days, 1), :]
    for k in range(1, days):
        part = part + contracted[k] * day_ref[pl.ds(day_index * days + k, 1), :]
    piece = slots // 8
    for i in range(8):
        slot_part[i] = part[i * piece : (i + 1) * piece]

    def device_8(p):
        return device(z, p // 2, x_hi * 2 + lax.rem(p, 2), core)

    me_8 = y * 2 + day_index
    s8 = Exchange((s8_buf, s8_s, s8_r), 8, me_8, device_8, slot_part)
    sz = Exchange((sz_buf, sz_s, sz_r), NZ, z, device_z)
    sa = Exchange((sa_buf, sa_s, sa_r), 32, me_32, device_32)
    s8.start()
    s8_buf[me_8] = slot_part[me_8]

    for p in range(NY):
        for k in range(days):
            for m in range(strips):
                row = (p * strips + m) * strip
                con_part[p, k * strips + m] = contracted[k][row : row + strip]
        for i in range(days * strips, NZ):
            con_part[p, i] = jnp.zeros((strip, R), f32)
    cy = Exchange((cy_buf, cy_s, cy_r), NY, y, device_y, con_part)
    cz = Exchange((cz_buf, cz_s, cz_r), NZ, z, device_z, con_rows)
    ca = Exchange((ca_buf, ca_s, ca_r), NZ, z, device_z)
    cy.start()
    cy_buf[y] = con_part[y]

    s8.wait_recv()
    sz_buf[z] = s8.total()
    sz.start()

    cy.wait_recv()
    con_rows[...] = cy.total()
    cz.start()
    cz_buf[z] = con_rows[z]

    gz.wait_recv()
    ga_buf[me_32] = gz.total()
    ga.start()
    sz.wait_recv()
    sa_buf[me_32] = sz.total()
    sa.start()
    cz.wait_recv()
    ca_buf[z] = cz.total()
    ca.start()
    ga.wait_recv()
    gram = jnp.concatenate([ga_buf[i * GROUP + g] for g in range(GROUP) for i in range(NY)], axis=0)

    def norms_of(gram, count):
        square = jnp.where(diagonal_mask(), gram, 0.0)
        row = jnp.sqrt(jnp.sum(square, axis=0, keepdims=True) / count + epsilon)
        column = jnp.sqrt(jnp.sum(square, axis=1, keepdims=True) / count + epsilon)
        return row, gram / (column * row)

    sensor_norms, gram_sensor = norms_of(gram, sensor_count)
    sensor_out[...] = gathered[me, rows_of(me), :] / sensor_norms
    inv_slot = inverse(regularize(gram_sensor * gram_day))

    sa.wait_recv()
    slot_rhs = [sa_buf[(i // 2) * 8 + s * 2 + i % 2] for s in range(4) for i in range(8)]
    slot_rhs = jnp.concatenate(slot_rhs, axis=0) / sensor_norms
    slot_all[...] = dot(slot_rhs, inv_slot, precision=highest)
    gram = gram_of(slot_all[...])
    slot_norms, gram_slot_new = norms_of(gram, slot_count)
    slot_new = slot_all[pl.ds(pl.multiple_of(slot_index * slots, 8), slots), :] / slot_norms
    slot_out[...] = slot_new

    weight = slot_new / sensor_norms
    for i in range(NY * strips):
        weights[i] = weight[i * strip : (i + 1) * strip]
    ca.wait_recv()
    for k in range(days):
        total = ca_buf[k * strips] * weights[y * strips]
        for m in range(1, strips):
            total = total + ca_buf[k * strips + m] * weights[y * strips + m]
        dy_buf[y * 4 + slot_index, k : k + 1] = jnp.sum(total, axis=0, keepdims=True)

    def device_16(p):
        return (z * NY + p // 4, lax.rem(p, 4), day_index)

    me_16 = y * 4 + slot_index
    dy = Exchange((dy_buf, dy_s, dy_r), 16, me_16, device_16)
    dy.start()
    inv_day = inverse(regularize(gram_sensor * gram_slot_new))
    dy.wait_recv()
    day_out[...] = dot(dy.total(), inv_day, precision=highest)

    def drain(j, carry):
        sibling_copy(j).wait_send()
        for h in range(2):
            forward_copy(j, h, True).wait_send()

        @pl.when(j < NX - 1)
        def _():
            for h in range(2):
                x_copy(j, h).wait_send()
                gather_copy(j, h, True).wait_send()

        return carry

    lax.fori_loop(0, NX, drain, 0)
    for exchange in (gx, gy, gz, ga, s8, sz, sa, cy, cz, ca, dy):
        exchange.wait_send()


def on_device(traffic, slot_factor, day_factor):
    days, slots, sensors = traffic.shape
    slot_count = slot_factor.shape[0]
    sensor_count = sensors * lax.axis_size("sensor")
    own = sensors // GROUP
    padded = (days * slots + 15) // 16 * 16
    strip = slots // NY // (NZ // days)

    def exchange_scratch(count, *block):
        return [
            pltpu.VMEM((count, *block), f32),
            pltpu.SemaphoreType.DMA((count,)),
            pltpu.SemaphoreType.DMA((count,)),
        ]

    dma = pltpu.SemaphoreType.DMA
    scratch = [
        pltpu.VMEM(slot_factor.shape, f32),
        pltpu.VMEM(day_factor.shape, f32),
        pltpu.VMEM((GROUP, days, slots, WINDOW), f32),
        pltpu.VMEM((GROUP, padded, WINDOW), bf16),
        pltpu.VMEM((GROUP, padded, WINDOW), bf16),
        pltpu.VMEM((padded, 2 * R), bf16),
        dma((2,)),
        dma((GROUP,)),
        pltpu.VMEM((NX, WINDOW, R), f32),
        pltpu.VMEM((NX, WINDOW, R), f32),
        *exchange_scratch(NX, own, R),
        pltpu.VMEM((NX, own, R), f32),
        pltpu.VMEM((NX - 1, own, R), f32),
        dma((NX - 1, 2)), dma((NX - 1, 2)),
        pltpu.VMEM((GROUP, WINDOW, R), f32),
        dma((NX - 1, 2)), dma((NX - 1, 2)), dma((NX, 2)), dma((NX, 2)),
        pltpu.VMEM((padded, 2 * R), f32),
        pltpu.VMEM((padded, R), f32),
        pltpu.VMEM((GROUP, 16, R), f32),
        pltpu.VMEM((NY, 4, R), f32),
        *exchange_scratch(GROUP, 16, R),
        *exchange_scratch(NY, 4, R),
        *exchange_scratch(NZ, 4, R),
        *exchange_scratch(32, 4, R),
        pltpu.VMEM((8, slots // 8, R), f32),
        *exchange_scratch(8, slots // 8, R),
        *exchange_scratch(NZ, slots // 8, R),
        *exchange_scratch(32, slots // 8, R),
        pltpu.VMEM(slot_factor.shape, f32),
        pltpu.VMEM((NY, NZ, strip, R), f32),
        pltpu.VMEM((NZ, strip, R), f32),
        *exchange_scratch(NY, NZ, strip, R),
        *exchange_scratch(NZ, strip, R),
        *exchange_scratch(NZ, strip, R),
        pltpu.VMEM((slots // strip, strip, R), f32),
        *exchange_scratch(16, days, R),
    ]
    vmem = pl.BlockSpec(memory_space=pltpu.VMEM)

    def kernel(*refs):
        body(sensor_count, slot_count, *refs)

    results = pl.pallas_call(
        kernel,
        out_shape=(
            jax.ShapeDtypeStruct((own, R), f32),
            jax.ShapeDtypeStruct((slots, R), f32),
            jax.ShapeDtypeStruct((days, R), f32),
        ),
        in_specs=[pl.BlockSpec(memory_space=pltpu.HBM)] * 3,
        out_specs=(vmem, vmem, vmem),
        scratch_shapes=scratch,
        compiler_params=pltpu.CompilerParams(
            collective_id=0, has_side_effects=True, vmem_limit_bytes=60 * 1024 * 1024
        ),
    )(traffic, slot_factor, day_factor)

    def store(*refs):
        for i in range(3):
            refs[3 + i][...] = refs[i][...]

    return pl.pallas_call(
        store,
        out_shape=tuple(jax.ShapeDtypeStruct(a.shape, f32) for a in results),
        in_specs=[vmem] * 3,
        out_specs=(vmem,) * 3,
    )(*results)


def solution(mesh):
    in_specs = (P("day", "slot", "sensor"), P(), P())
    out_specs = (P(("sensor", "slot", "day"), None), P("slot", None), P("day", None))
    return jax.shard_map(
        on_device, mesh=mesh, in_specs=in_specs, out_specs=out_specs, check_vma=False
    )
```

time: 99.9 us -> 78.8 us (0.79)
  Pallas kernels: 93.3 us -> 77.8 us
  local copies, waits for them, and re-layouts: 5.79 us -> 0 us
    pallas_call x1, Pallas kernels: 93.3 us -> 76.2 us  [on_device(): pl.pallas_call(kernel, out_shape=(jax.ShapeDtypeStruct((own, R), f32), ja...]
    unnamed x9 -> x0, local copies, waits for them, and re-layouts: 5.79 us -> none
    pallas_call x0 -> x1, Pallas kernels: none -> 1.65 us  [on_device(): pl.pallas_call(store, out_shape=tuple((jax.ShapeDtypeStruct(a.shape, f32)...]
where the time goes in v2:
time: 78.8 us; the launch traced here: 78.5 us
  Pallas kernels  77.8 us (99%)
    pallas_call x1, Pallas kernels, on_device(): pl.pallas_call(kernel, out_shape=(jax.ShapeDtypeStruct((own, R), f32), ja...  76.2 us
    pallas_call x1, Pallas kernels, on_device(): pl.pallas_call(store, out_shape=tuple((jax.ShapeDtypeStruct(a.shape, f32)...  1.65 us

profile of v2, /device:TPU:1, one launch (start us, length us, event | category | flops | bytes accessed | tf_op | source)
XLA Modules:
  0.0 78.5 jit_solution(15987621621550233713)
XLA Ops:
  0.6 76.2 %shard_map.58 = (f32[400,128]{1,0:T(8,128)}, f32[72,128]{1,0:T(8,128)}, f32[5,128]{1,0:T(8,128)}) custom-call(f32[5,72,3200]{2,1,0:T(8,128)} %refs_0_.1, f32[288,128]{1,0:T(8,128)} %refs_1_.1, f32[10,128]{1,0:T(8,128)} %refs_2_.1), custom_call_target="tpu_custom_call" | custom-call | tf_op jit(solution)/shard_map/pallas_call | solution.py:572
  76.8 1.7 %shard_map.59 = (f32[400,128]{1,0:T(8,128)}, f32[72,128]{1,0:T(8,128)}, f32[5,128]{1,0:T(8,128)}) custom-call(f32[400,128]{1,0:T(8,128)} %get-tuple-element.6.refs_0_, f32[72,128]{1,0:T(8,128)} %get-tuple-element.7.refs_1_, f32[5,128]{1,0:T(8,128)} %get-tuple-element.8.refs_2_), custom_call_target="tpu_custom_call" | custom-call | tf_op jit(solution)/shard_map/pallas_call | solution.py:591

commit v3 on v2

--- a/solution.py
+++ b/solution.py
@@ -120,7 +120,7 @@
 def body(
     sensor_count, slot_count,
     traffic, slot_in, day_in, sensor_out, slot_out, day_out,
-    slot_ref, day_ref, t_win, t_high, t_low, w_cat, factor_sem, load_sem,
+    slot_ref, day_ref, t_win, t_high, t_low, w_cat, factor_sem, load_sem, round_sem,
     win_sib, win_own, sib_recv, sib_ssem, sib_rsem, x_send, x_recv, x_ssem, x_rsem,
     gathered, gat_ssem, gat_rsem, fwd_ssem, fwd_rsem,
     c_wide, c_low,
@@ -163,22 +163,17 @@
         greet(group_device(lax.rem(me + k, GROUP)))
         return carry
 
-    def greet_z(k, carry):
+    lax.fori_loop(1, GROUP, greet_group, 0)
+    for k in range(1, NY):
+        greet(device(z, lax.rem(y + k, NY), x, core))
+    for k in (1, NZ - 1):
         greet(device(lax.rem(z + k, NZ), y, x, core))
-        return carry
-
-    def greet_y(k, carry):
-        other = lax.rem(y + k, NY)
-        for cx, cc in ((0, 0), (0, 1), (2, 0), (2, 1), (None, 0)):
-            if cx is None:
-                greet(device(z, other, x_hi * 2 + 1 - day_index, core))
-            else:
-                greet(device(z, other, lax.rem(x + cx, NX), lax.rem(core + cc, 2)))
-        return carry
-
-    lax.fori_loop(1, GROUP, greet_group, 0)
-    lax.fori_loop(1, NZ, greet_z, 0)
-    lax.fori_loop(1, NY, greet_y, 0)
+    barrier_count = (GROUP - 1) + (NY - 1) + 2
+
+    def round_z(i):
+        for k in (2**i, NZ - 2**i):
+            target = device(lax.rem(z + k, NZ), y, x, core)
+            pl.semaphore_signal(round_sem.at[i], inc=1, device_id=target, device_id_type=MESH)
 
     factor_loads = [
         pltpu.make_async_copy(slot_in, slot_ref, factor_sem.at[0]),
@@ -259,7 +254,8 @@
 
             @pl.when(j == 0)
             def _():
-                pl.semaphore_wait(barrier, 7 + (NZ - 1) + 5 * (NY - 1))
+                pl.semaphore_wait(barrier, barrier_count)
+                round_z(0)
 
             sibling_copy(j).start()
 
@@ -278,6 +274,8 @@
     for j in range(NX - 1):
         x_copy(j, 1).start()
 
+    pl.semaphore_wait(round_sem.at[0], 2)
+    round_z(1)
     gram_day = gram_of(day_ref[...])
     inv_sensor = inverse(regularize(gram_of(slot_ref[...]) * gram_day))
 
@@ -329,6 +327,8 @@
             gather_copy(j, h, True).start()
         forward_copy(3, h, True).start()
 
+    pl.semaphore_wait(round_sem.at[1], 2)
+    round_z(2)
     gram = own_half(0)
     gather_start(0)
     gram = gram + own_half(1)
@@ -337,6 +337,7 @@
     gx.start()
     gx_buf[me] = gram_part[me]
     gather_start(1)
+    pl.semaphore_wait(round_sem.at[2], 2)
 
     def second_product(chunk):
         high, low = split(gathered[chunk])
@@ -535,6 +536,7 @@
         pltpu.VMEM((padded, 2 * R), bf16),
         dma((2,)),
         dma((GROUP,)),
+        pltpu.SemaphoreType.REGULAR((3,)),
         pltpu.VMEM((NX, WINDOW, R), f32),
         pltpu.VMEM((NX, WINDOW, R), f32),
         *exchange_scratch(NX, own, R),

time: 78.8 us -> 76.6 us (0.972)
  Pallas kernels: 77.8 us -> 75.7 us
    pallas_call x1, Pallas kernels: 76.2 us -> 74.1 us  [on_device(): pl.pallas_call(kernel, out_shape=(jax.ShapeDtypeStruct((own, R), f32), ja...]
where the time goes in v3:
time: 76.6 us; the launch traced here: 76.4 us
  Pallas kernels  75.7 us (99%)
    pallas_call x1, Pallas kernels, on_device(): pl.pallas_call(kernel, out_shape=(jax.ShapeDtypeStruct((own, R), f32), ja...  74.1 us
    pallas_call x1, Pallas kernels, on_device(): pl.pallas_call(store, out_shape=tuple((jax.ShapeDtypeStruct(a.shape, f32)...  1.65 us

profile of v3, /device:TPU:1, one launch (start us, length us, event | category | flops | bytes accessed | tf_op | source)
XLA Modules:
  0.0 76.4 jit_solution(3360057686403537364)
XLA Ops:
  0.6 74.1 %shard_map.58 = (f32[400,128]{1,0:T(8,128)}, f32[72,128]{1,0:T(8,128)}, f32[5,128]{1,0:T(8,128)}) custom-call(f32[5,72,3200]{2,1,0:T(8,128)} %refs_0_.1, f32[288,128]{1,0:T(8,128)} %refs_1_.1, f32[10,128]{1,0:T(8,128)} %refs_2_.1), custom_call_target="tpu_custom_call" | custom-call | tf_op jit(solution)/shard_map/pallas_call | solution.py:574
  74.7 1.7 %shard_map.59 = (f32[400,128]{1,0:T(8,128)}, f32[72,128]{1,0:T(8,128)}, f32[5,128]{1,0:T(8,128)}) custom-call(f32[400,128]{1,0:T(8,128)} %get-tuple-element.6.refs_0_, f32[72,128]{1,0:T(8,128)} %get-tuple-element.7.refs_1_, f32[5,128]{1,0:T(8,128)} %get-tuple-element.8.refs_2_), custom_call_target="tpu_custom_call" | custom-call | tf_op jit(solution)/shard_map/pallas_call | solution.py:593

commit v4 on v3

--- a/solution.py
+++ b/solution.py
@@ -80,35 +80,30 @@
         self.buffer, self.send_sem, self.recv_sem = refs
         self.count, self.me, self.device, self.source = count, me, device, source
 
-    def copy(self, k, slot):
-        peer = lax.rem(self.me + k, self.count)
-        source = self.buffer.at[self.me] if self.source is None else self.source.at[peer]
+    def start(self):
+        middle = self.count // 2
+        for i in range(self.count - 1):
+            k = middle + (i + 1) // 2 if i % 2 else middle - i // 2
+            peer = lax.rem(self.me + k, self.count)
+            source = self.buffer.at[self.me] if self.source is None else self.source.at[peer]
+            pltpu.make_async_remote_copy(
+                src_ref=source, dst_ref=self.buffer.at[self.me],
+                send_sem=self.send_sem, recv_sem=self.recv_sem,
+                device_id=self.device(peer), device_id_type=MESH,
+            ).start()
+
+    def all_copies(self):
+        part = self.buffer.at[pl.ds(0, self.count - 1)]
         return pltpu.make_async_remote_copy(
-            src_ref=source,
-            dst_ref=self.buffer.at[self.me if slot is None else peer],
-            send_sem=self.send_sem.at[k],
-            recv_sem=self.recv_sem.at[self.me if slot is None else peer],
-            device_id=self.device(peer),
-            device_id_type=MESH,
+            src_ref=part, dst_ref=part, send_sem=self.send_sem, recv_sem=self.recv_sem,
+            device_id=self.device(lax.rem(self.me + 1, self.count)), device_id_type=MESH,
         )
 
-    def each(self, act):
-        middle = self.count // 2
-
-        def step(i, carry):
-            act(middle + jnp.where(lax.rem(i, 2) == 1, (i + 1) // 2, -(i // 2)))
-            return carry
-
-        lax.fori_loop(0, self.count - 1, step, 0)
-
-    def start(self):
-        self.each(lambda k: self.copy(k, None).start())
-
     def wait_recv(self):
-        self.each(lambda k: self.copy(k, "peer").wait_recv())
+        self.all_copies().wait_recv()
 
     def wait_send(self):
-        self.each(lambda k: self.copy(k, None).wait_send())
+        self.all_copies().wait_send()
 
     def total(self):
         total = self.buffer[0]
@@ -121,6 +116,7 @@
     sensor_count, slot_count,
     traffic, slot_in, day_in, sensor_out, slot_out, day_out,
     slot_ref, day_ref, t_win, t_high, t_low, w_cat, factor_sem, load_sem, round_sem,
+    sensor_stage, slot_stage, day_stage, out_sem,
     win_sib, win_own, sib_recv, sib_ssem, sib_rsem, x_send, x_recv, x_ssem, x_rsem,
     gathered, gat_ssem, gat_rsem, fwd_ssem, fwd_rsem,
     c_wide, c_low,
@@ -175,6 +171,10 @@
             target = device(lax.rem(z + k, NZ), y, x, core)
             pl.semaphore_signal(round_sem.at[i], inc=1, device_id=target, device_id_type=MESH)
 
+    out_copies = [
+        pltpu.make_async_copy(source, target, out_sem.at[i])
+        for i, (source, target) in enumerate(((sensor_stage, sensor_out), (slot_stage, slot_out), (day_stage, day_out)))
+    ]
     factor_loads = [
         pltpu.make_async_copy(slot_in, slot_ref, factor_sem.at[0]),
         pltpu.make_async_copy(day_in, day_ref, factor_sem.at[1]),
@@ -433,6 +433,16 @@
     cy.start()
     cy_buf[y] = con_part[y]
 
+    for j in range(NX):
+        sibling_copy(j).wait_send()
+        for h in range(2):
+            forward_copy(j, h, True).wait_send()
+            if j < NX - 1:
+                x_copy(j, h).wait_send()
+                gather_copy(j, h, True).wait_send()
+    gx.wait_send()
+    gy.wait_send()
+
     s8.wait_recv()
     sz_buf[z] = s8.total()
     sz.start()
@@ -445,12 +455,11 @@
     gz.wait_recv()
     ga_buf[me_32] = gz.total()
     ga.start()
+    for exchange in (gz, s8, cy, sz):
+        exchange.wait_send()
     sz.wait_recv()
     sa_buf[me_32] = sz.total()
     sa.start()
-    cz.wait_recv()
-    ca_buf[z] = cz.total()
-    ca.start()
     ga.wait_recv()
     gram = jnp.concatenate([ga_buf[i * GROUP + g] for g in range(GROUP) for i in range(NY)], axis=0)
 
@@ -461,9 +470,15 @@
         return row, gram / (column * row)
 
     sensor_norms, gram_sensor = norms_of(gram, sensor_count)
-    sensor_out[...] = gathered[me, rows_of(me), :] / sensor_norms
+    sensor_stage[...] = gathered[me, rows_of(me), :] / sensor_norms
+    out_copies[0].start()
+    cz.wait_recv()
+    ca_buf[z] = cz.total()
+    ca.start()
     inv_slot = inverse(regularize(gram_sensor * gram_day))
 
+    ga.wait_send()
+    cz.wait_send()
     sa.wait_recv()
     slot_rhs = [sa_buf[(i // 2) * 8 + s * 2 + i % 2] for s in range(4) for i in range(8)]
     slot_rhs = jnp.concatenate(slot_rhs, axis=0) / sensor_norms
@@ -471,11 +486,13 @@
     gram = gram_of(slot_all[...])
     slot_norms, gram_slot_new = norms_of(gram, slot_count)
     slot_new = slot_all[pl.ds(pl.multiple_of(slot_index * slots, 8), slots), :] / slot_norms
-    slot_out[...] = slot_new
+    slot_stage[...] = slot_new
+    out_copies[1].start()
 
     weight = slot_new / sensor_norms
     for i in range(NY * strips):
         weights[i] = weight[i * strip : (i + 1) * strip]
+    sa.wait_send()
     ca.wait_recv()
     for k in range(days):
         total = ca_buf[k * strips] * weights[y * strips]
@@ -490,25 +507,14 @@
     dy = Exchange((dy_buf, dy_s, dy_r), 16, me_16, device_16)
     dy.start()
     inv_day = inverse(regularize(gram_sensor * gram_slot_new))
+    ca.wait_send()
     dy.wait_recv()
-    day_out[...] = dot(dy.total(), inv_day, precision=highest)
-
-    def drain(j, carry):
-        sibling_copy(j).wait_send()
-        for h in range(2):
-            forward_copy(j, h, True).wait_send()
-
-        @pl.when(j < NX - 1)
-        def _():
-            for h in range(2):
-                x_copy(j, h).wait_send()
-                gather_copy(j, h, True).wait_send()
-
-        return carry
-
-    lax.fori_loop(0, NX, drain, 0)
-    for exchange in (gx, gy, gz, ga, s8, sz, sa, cy, cz, ca, dy):
-        exchange.wait_send()
+    day_stage[...] = dot(dy.total(), inv_day, precision=highest)
+    out_copies[2].start()
+    for copy in out_copies:
+        copy.wait()
+
+    dy.wait_send()
 
 
 def on_device(traffic, slot_factor, day_factor):
@@ -522,8 +528,8 @@
     def exchange_scratch(count, *block):
         return [
             pltpu.VMEM((count, *block), f32),
-            pltpu.SemaphoreType.DMA((count,)),
-            pltpu.SemaphoreType.DMA((count,)),
+            pltpu.SemaphoreType.DMA,
+            pltpu.SemaphoreType.DMA,
         ]
 
     dma = pltpu.SemaphoreType.DMA
@@ -537,9 +543,14 @@
         dma((2,)),
         dma((GROUP,)),
         pltpu.SemaphoreType.REGULAR((3,)),
+        pltpu.VMEM((own, R), f32),
+        pltpu.VMEM((slots, R), f32),
+        pltpu.VMEM((days, R), f32),
+        dma((3,)),
         pltpu.VMEM((NX, WINDOW, R), f32),
         pltpu.VMEM((NX, WINDOW, R), f32),
-        *exchange_scratch(NX, own, R),
+        pltpu.VMEM((NX, own, R), f32),
+        dma((NX,)), dma((NX,)),
         pltpu.VMEM((NX, own, R), f32),
         pltpu.VMEM((NX - 1, own, R), f32),
         dma((NX - 1, 2)), dma((NX - 1, 2)),
@@ -579,7 +590,7 @@
             jax.ShapeDtypeStruct((days, R), f32),
         ),
         in_specs=[pl.BlockSpec(memory_space=pltpu.HBM)] * 3,
-        out_specs=(vmem, vmem, vmem),
+        out_specs=(pl.BlockSpec(memory_space=pl.ANY),) * 3,
         scratch_shapes=scratch,
         compiler_params=pltpu.CompilerParams(
             collective_id=0, has_side_effects=True, vmem_limit_bytes=60 * 1024 * 1024

time: 76.6 us -> 68.1 us (0.89)
  Pallas kernels: 75.7 us -> 67.3 us
    pallas_call x1, Pallas kernels: 74.1 us -> 65.6 us  [on_device(): pl.pallas_call(kernel, out_shape=(jax.ShapeDtypeStruct((own, R), f32), ja...]
where the time goes in v4:
time: 68.1 us; the launch traced here: 67.9 us
  Pallas kernels  67.3 us (99%)
    pallas_call x1, Pallas kernels, on_device(): pl.pallas_call(kernel, out_shape=(jax.ShapeDtypeStruct((own, R), f32), ja...  65.6 us
    pallas_call x1, Pallas kernels, on_device(): pl.pallas_call(store, out_shape=tuple((jax.ShapeDtypeStruct(a.shape, f32)...  1.65 us

profile of v4, /device:TPU:1, one launch (start us, length us, event | category | flops | bytes accessed | tf_op | source)
XLA Modules:
  0.0 67.9 jit_solution(2614904751705726312)
XLA Ops:
  0.6 65.6 %shard_map.58 = (f32[400,128]{1,0:T(8,128)}, f32[72,128]{1,0:T(8,128)}, f32[5,128]{1,0:T(8,128)}) custom-call(f32[5,72,3200]{2,1,0:T(8,128)} %refs_0_.1, f32[288,128]{1,0:T(8,128)} %refs_1_.1, f32[10,128]{1,0:T(8,128)} %refs_2_.1), custom_call_target="tpu_custom_call" | custom-call | tf_op jit(solution)/shard_map/pallas_call | solution.py:585
  66.3 1.7 %shard_map.59 = (f32[400,128]{1,0:T(8,128)}, f32[72,128]{1,0:T(8,128)}, f32[5,128]{1,0:T(8,128)}) custom-call(f32[400,128]{1,0:T(8,128)} %get-tuple-element.6.refs_0_, f32[72,128]{1,0:T(8,128)} %get-tuple-element.7.refs_1_, f32[5,128]{1,0:T(8,128)} %get-tuple-element.8.refs_2_), custom_call_target="tpu_custom_call" | custom-call | tf_op jit(solution)/shard_map/pallas_call | solution.py:604

commit v5 on v4

--- a/solution.py
+++ b/solution.py
@@ -134,19 +134,19 @@
     sensor_index = lax.axis_index("sensor")
     slot_index = lax.axis_index("slot")
     day_index = lax.axis_index("day")
-    z, y = sensor_index // NY, lax.rem(sensor_index, NY)
+    z, y = lax.div(sensor_index, NY), lax.rem(sensor_index, NY)
     core = lax.rem(slot_index, 2)
-    x_hi = slot_index // 2
+    x_hi = lax.div(slot_index, 2)
     x = x_hi * 2 + day_index
 
     def device(z, y, x, core):
-        return (z * NY + y, (x // 2) * 2 + core, lax.rem(x, 2))
+        return (z * NY + y, lax.div(x, 2) * 2 + core, lax.rem(x, 2))
 
     def chunk_of(x, core):
-        return ((x // 2) * 2 + core) * 2 + lax.rem(x, 2)
+        return (lax.div(x, 2) * 2 + core) * 2 + lax.rem(x, 2)
 
     def group_device(index):
-        return (sensor_index, index // 2, lax.rem(index, 2))
+        return (sensor_index, lax.div(index, 2), lax.rem(index, 2))
 
     me = chunk_of(x, core)
 
@@ -250,14 +250,13 @@
         @pl.when(j < NX)
         def _():
             first_product(chunk_of(target_x(j), 1 - core), win_sib.at[j])
-            first_product(chunk_of(target_x(j), core), win_own.at[j])
-
             @pl.when(j == 0)
             def _():
                 pl.semaphore_wait(barrier, barrier_count)
                 round_z(0)
 
             sibling_copy(j).start()
+            first_product(chunk_of(target_x(j), core), win_own.at[j])
 
         @pl.when(j > 0)
         def _():
@@ -286,16 +285,16 @@
             total = total + x_recv[j, h * half : (h + 1) * half]
         sensor_raw = dot(total, inv_sensor, precision=highest)
         gathered[me, half_rows_of(me, h), :] = sensor_raw
-        return gram_of(sensor_raw)
+        return sensor_raw
 
     def device_y(p):
-        return device(z, p, x, core)
+        return (z * NY + p, slot_index, day_index)
 
     def device_z(p):
-        return device(p, y, x, core)
+        return (p * NY + y, slot_index, day_index)
 
     def device_32(p):
-        return (z * NY + p // 8, lax.rem(p // 2, 4), lax.rem(p, 2))
+        return (z * NY + lax.div(p, 8), lax.rem(lax.div(p, 2), 4), lax.rem(p, 2))
 
     me_32 = y * 8 + me
     gx = Exchange((gx_buf, gx_s, gx_r), GROUP, me, group_device, gram_part)
@@ -329,9 +328,9 @@
 
     pl.semaphore_wait(round_sem.at[1], 2)
     round_z(2)
-    gram = own_half(0)
+    first_half = own_half(0)
     gather_start(0)
-    gram = gram + own_half(1)
+    gram = gram_of(first_half) + gram_of(own_half(1))
     for i in range(GROUP):
         gram_part[i] = gram[16 * i : 16 * i + 16]
     gx.start()
@@ -411,7 +410,7 @@
         slot_part[i] = part[i * piece : (i + 1) * piece]
 
     def device_8(p):
-        return device(z, p // 2, x_hi * 2 + lax.rem(p, 2), core)
+        return (z * NY + lax.div(p, 2), slot_index, lax.rem(p, 2))
 
     me_8 = y * 2 + day_index
     s8 = Exchange((s8_buf, s8_s, s8_r), 8, me_8, device_8, slot_part)
@@ -501,7 +500,7 @@
         dy_buf[y * 4 + slot_index, k : k + 1] = jnp.sum(total, axis=0, keepdims=True)
 
     def device_16(p):
-        return (z * NY + p // 4, lax.rem(p, 4), day_index)
+        return (z * NY + lax.div(p, 4), lax.rem(p, 4), day_index)
 
     me_16 = y * 4 + slot_index
     dy = Exchange((dy_buf, dy_s, dy_r), 16, me_16, device_16)

time: 68.1 us -> 67.7 us (level)
  no operation moved by 1% of the time
where the time goes in v5:
time: 67.7 us; the launch traced here: 67.6 us
  Pallas kernels  67 us (99%)
    pallas_call x1, Pallas kernels, on_device(): pl.pallas_call(kernel, out_shape=(jax.ShapeDtypeStruct((own, R), f32), ja...  65.3 us
    pallas_call x1, Pallas kernels, on_device(): pl.pallas_call(store, out_shape=tuple((jax.ShapeDtypeStruct(a.shape, f32)...  1.65 us

profile of v5, /device:TPU:1, one launch (start us, length us, event | category | flops | bytes accessed | tf_op | source)
XLA Modules:
  0.0 67.6 jit_solution(15300347962660696856)
XLA Ops:
  0.6 65.3 %shard_map.58 = (f32[400,128]{1,0:T(8,128)}, f32[72,128]{1,0:T(8,128)}, f32[5,128]{1,0:T(8,128)}) custom-call(f32[5,72,3200]{2,1,0:T(8,128)} %refs_0_.1, f32[288,128]{1,0:T(8,128)} %refs_1_.1, f32[10,128]{1,0:T(8,128)} %refs_2_.1), custom_call_target="tpu_custom_call" | custom-call | tf_op jit(solution)/shard_map/pallas_call | solution.py:584
  65.9 1.7 %shard_map.59 = (f32[400,128]{1,0:T(8,128)}, f32[72,128]{1,0:T(8,128)}, f32[5,128]{1,0:T(8,128)}) custom-call(f32[400,128]{1,0:T(8,128)} %get-tuple-element.6.refs_0_, f32[72,128]{1,0:T(8,128)} %get-tuple-element.7.refs_1_, f32[5,128]{1,0:T(8,128)} %get-tuple-element.8.refs_2_), custom_call_target="tpu_custom_call" | custom-call | tf_op jit(solution)/shard_map/pallas_call | solution.py:603

commit v6 on v5

--- a/solution.py
+++ b/solution.py
@@ -445,15 +445,15 @@
     s8.wait_recv()
     sz_buf[z] = s8.total()
     sz.start()
+    gz.wait_recv()
+    ga_buf[me_32] = gz.total()
+    ga.start()
 
     cy.wait_recv()
     con_rows[...] = cy.total()
     cz.start()
     cz_buf[z] = con_rows[z]
 
-    gz.wait_recv()
-    ga_buf[me_32] = gz.total()
-    ga.start()
     for exchange in (gz, s8, cy, sz):
         exchange.wait_send()
     sz.wait_recv()

time: 67.7 us -> 67.5 us (level)
  no operation moved by 1% of the time
where the time goes in v6:
time: 67.5 us; the launch traced here: 67.4 us
  Pallas kernels  66.8 us (99%)
    pallas_call x1, Pallas kernels, on_device(): pl.pallas_call(kernel, out_shape=(jax.ShapeDtypeStruct((own, R), f32), ja...  65.1 us
    pallas_call x1, Pallas kernels, on_device(): pl.pallas_call(store, out_shape=tuple((jax.ShapeDtypeStruct(a.shape, f32)...  1.65 us

profile of v6, /device:TPU:1, one launch (start us, length us, event | category | flops | bytes accessed | tf_op | source)
XLA Modules:
  0.0 67.4 jit_solution(1718318038779015492)
XLA Ops:
  0.6 65.1 %shard_map.58 = (f32[400,128]{1,0:T(8,128)}, f32[72,128]{1,0:T(8,128)}, f32[5,128]{1,0:T(8,128)}) custom-call(f32[5,72,3200]{2,1,0:T(8,128)} %refs_0_.1, f32[288,128]{1,0:T(8,128)} %refs_1_.1, f32[10,128]{1,0:T(8,128)} %refs_2_.1), custom_call_target="tpu_custom_call" | custom-call | tf_op jit(solution)/shard_map/pallas_call | solution.py:584
  65.8 1.7 %shard_map.59 = (f32[400,128]{1,0:T(8,128)}, f32[72,128]{1,0:T(8,128)}, f32[5,128]{1,0:T(8,128)}) custom-call(f32[400,128]{1,0:T(8,128)} %get-tuple-element.6.refs_0_, f32[72,128]{1,0:T(8,128)} %get-tuple-element.7.refs_1_, f32[5,128]{1,0:T(8,128)} %get-tuple-element.8.refs_2_), custom_call_target="tpu_custom_call" | custom-call | tf_op jit(solution)/shard_map/pallas_call | solution.py:603
